TPU v7x, 32 devices: a whole 2x2x4 slice. The times are simulated.
32 devices in a mesh: ao: 4 (over z), mo: 8 (over y, x, core).
Axes of the slice: x: 2, y: 2, z: 4, core: 2. Of those that a mesh axis runs over, the one named last changes fastest.
Arguments:
- pair_ints: bfloat16 [32, 4096, 256], P(('ao', 'mo')), may hold values from -6 to 6
- shell_pairs: int32 [32, 2], replicated, may hold values from 0 to 31, as said below
- occ_lam: bfloat16 [16, 32], replicated, may hold values from -1.5 to 1.5
- occ_sig: bfloat16 [16, 4], replicated, may hold values from -1.5 to 1.5
- coef_act: bfloat16 [2048, 2048], P(None, 'mo'), may hold values from -0.1875 to 0.1875
- slabs: int32 [2], replicated, may hold values from 0 to 7, as said below
Outputs:
- mo_ints: bfloat16 [2, 4, 4, 2048, 2048], P(None, 'ao', None, 'mo')
Inputs may be any that keep to these rules, and one draw needn't show every extreme that they name: `shell_pairs`: each row holds two shell numbers P <= Q, no two rows are equal, and some row holds 0 and 31. `slabs`: the two slab numbers differ.
All inputs are finite; a program needn't handle non-finite values.
Results may differ from a plain program's by a relative error of at most 0.0066.
Values may be sent and summed in bfloat16 or wider, within the bound.
A program may use at most 128 MiB of HBM per device.

v0:
```python
import jax
import jax.numpy as jnp
from jax import lax
from jax.sharding import PartitionSpec as P

SH = 64
NSH = 32
ACT = 2048
KL = 16
KS = 16
NI = 4


def ket_transform(pair_ints, occ_lam, occ_sig, slab_index):
    blocks_here = pair_ints.shape[0]
    nj_all = occ_sig.shape[1]
    lam_cols = lax.dynamic_slice_in_dim(occ_lam, slab_index * NI, NI, 1).astype(jnp.float32)
    pair_coef = occ_sig.astype(jnp.float32).T[:, None, None, :] * lam_cols.T[None, :, :, None]
    pair_coef = pair_coef.reshape(nj_all * NI, KL * KS).astype(jnp.bfloat16)
    half_ints = jnp.einsum("bqw,xw->bxq", pair_ints, pair_coef, preferred_element_type=jnp.float32)
    return half_ints.astype(jnp.bfloat16).reshape(blocks_here, nj_all, NI, SH * SH)


def remap_pairs(stacked):
    owned = lax.all_to_all(stacked, "ao", split_axis=2, concat_axis=1, tiled=True)
    return lax.all_gather(owned, "mo", axis=1, tiled=True)


def body(pair_ints, shell_pairs, occ_lam, occ_sig, coef_act, slabs):
    ao_count = lax.axis_size("ao")
    mo_count = lax.axis_size("mo")
    blocks_here = pair_ints.shape[0]
    panel_width = coef_act.shape[1]
    ao_width = coef_act.shape[0]
    first_half = ket_transform(pair_ints, occ_lam, occ_sig, slabs[0])
    second_half = ket_transform(pair_ints, occ_lam, occ_sig, slabs[1])
    ordered_pairs = (
        shell_pairs.reshape(ao_count, mo_count, blocks_here, 2).transpose(1, 0, 2, 3).reshape(-1, 2)
    )
    gathered_slabs = [remap_pairs(single[None])[0] for single in (first_half, second_half)]
    coef_shells = coef_act.reshape(NSH, SH, panel_width)
    shell_numbers = jnp.arange(NSH, dtype=jnp.int32)

    def bra_transform(gathered):
        block_count = gathered.shape[0]
        pair_rows = gathered.shape[1] * gathered.shape[2]
        grouped = gathered.reshape(block_count // 16, 16, pair_rows, SH, SH)
        grouped_pairs = ordered_pairs.reshape(block_count // 16, 16, 2)

        def accumulate(running, group_item):
            block_vals, block_pairs = group_item
            shell_one = block_pairs[:, 0]
            shell_two = block_pairs[:, 1]
            coef_one = jnp.take(coef_shells, shell_one, axis=0)
            coef_two = jnp.take(coef_shells, shell_two, axis=0)
            term_one = jnp.einsum(
                "prmn,pma->pran", block_vals, coef_one, preferred_element_type=jnp.float32
            )
            term_two = jnp.einsum(
                "prmn,pna->pram", block_vals, coef_two, preferred_element_type=jnp.float32
            )
            differs = (shell_one != shell_two).astype(jnp.float32)
            place_two = (shell_two[:, None] == shell_numbers[None, :]).astype(jnp.float32)
            place_one = (shell_one[:, None] == shell_numbers[None, :]).astype(
                jnp.float32
            ) * differs[:, None]
            added = jnp.einsum(
                "ps,pran->rasn", place_two, term_one, precision=lax.Precision.HIGHEST
            )
            added = added + jnp.einsum(
                "ps,pram->rasm", place_one, term_two, precision=lax.Precision.HIGHEST
            )
            return (running + added, None)

        start_terms = jnp.zeros((pair_rows, panel_width, NSH, SH), jnp.float32)
        left_terms = lax.scan(accumulate, start_terms, (grouped, grouped_pairs))[0]
        left_rounded = left_terms.astype(jnp.bfloat16).reshape(pair_rows * panel_width, ao_width)
        product = jnp.dot(
            left_rounded,
            lax.all_gather(coef_act, "mo", axis=1, tiled=True),
            preferred_element_type=jnp.float32,
        )
        return product.astype(jnp.bfloat16).reshape(gathered.shape[1], NI, panel_width, ACT)

    results = [bra_transform(gathered) for gathered in gathered_slabs]
    return jnp.stack(results)


def solution(mesh):
    return jax.shard_map(
        body,
        mesh=mesh,
        in_specs=(P(("ao", "mo"), None, None), P(), P(), P(), P(None, "mo"), P()),
        out_specs=P(None, "ao", None, "mo", None),
        check_vma=False,
    )
```

profile of v0, /device:TPU:0, one launch (start us, length us, event | category | flops | bytes accessed | tf_op | source)
XLA Modules:
  0.0 232.0 jit_solution(11664202074742038208)
XLA Ops:
  12.0 12.4 %all_to_all.24 = bf16[1,1,4,4,4096]{4,3,1,0,2:T(4,128)(2,1)} all-to-all(bf16[1,1,4,4,4096]{4,3,1,0,2:T(4,128)(2,1)S(1)} %bitcast.198), channel_id=1, replica_groups=mesh['ao'=4,'mo'=8] {'ao'}, dimensions={2} | all-to-all | bytes 262144 | tf_op jit(solution)/shard_map/all_to_all | solution.py:25
  25.3 9.0 %all_to_all.25 = bf16[1,1,4,4,4096]{4,3,1,0,2:T(4,128)(2,1)} all-to-all(bf16[1,1,4,4,4096]{4,3,1,0,2:T(4,128)(2,1)S(1)} %bitcast.199), channel_id=1, replica_groups=mesh['ao'=4,'mo'=8] {'ao'}, dimensions={2} | all-to-all | bytes 262144 | tf_op jit(solution)/shard_map/all_to_all | solution.py:25
  35.3 11.8 %all-gather.10.cloned.1.call-done = bf16[1,1,32,4,4096]{4,3,1,0,2:T(4,128)(2,1)} async-done(((bf16[1,1,4,4,4096]{4,3,1,0,2:T(4,128)(2,1)}), bf16[1,1,32,4,4096]{4,3,1,0,2:T(4,128)(2,1)}) %all-gather.10.cloned.1.call-update) | async-done | bytes 1048592 | tf_op jit(solution)/shard_map/all_gather | solution.py:26
  47.2 4.3 %reshape_squeeze.7 = bf16[2,16,4,64,64]{4,3,2,1,0:T(8,128)(2,1)} reshape(bf16[1,1,32,4,4096]{4,3,1,0,2:T(4,128)(2,1)} %all-gather.10.cloned.1.call-done) | data formatting | bytes 2097152 | tf_op jit(solution)/shard_map/reshape;squeeze | solution.py:47
  51.5 66.0 %while.25 = (s32[]{:T(128)}, f32[4,256,32,64]{1,2,3,0:T(8,128)}, s32[2,16,2]{1,2,0:T(2,128)S(1)}, bf16[32,64,256]{2,1,0:T(8,128)(2,1)S(1)}, bf16[2,16,4,64,64]{4,3,2,1,0:T(8,128)(2,1)}, /*index=5*/s32[]{:T(128)}, s32[]{:T(128)}) while((s32[]{:T(128)}, f32[4,256,32,64]{1,2,3,0:T(8,128)}, s32[2,16,2]{1,2,0:T(2,128)S(1)}, ...), condition=%wide.region_3.5_spmd.clone.clone, body=%wide.region_2.4_spmd.clone.clone.sunk | while | flops 1080561408 | bytes 58730048 | solution.py:76
  59.2 9.1 %fusion.111 = f32[4,256,64,32]{1,3,2,0:T(8,128)S(1)} fusion(f32[16,4,256,64]{2,3,1,0:T(8,128)S(1)} %convolution_bitcast_fusion.5, f32[16]{0:T(128)S(1)} %fusion.110, s32[16]{0:T(128)S(1)} %get-tuple-element.316), kind=kOutput, calls=%fused_computation.46.clone.1 | convolution fusion | flops 402654208 | bytes 12583040 | tf_op jit(solution)/shard_map/while/body/eval_jaxpr/ps,pram->rasm/dot_general | solution.py:70
  68.4 8.1 %bitcast_add_fusion.5 = f32[4,256,32,64]{1,2,3,0:T(8,128)} fusion(f32[4,256,32,64]{1,2,3,0:T(8,128)} %get-tuple-element.328, f32[4,256,64,32]{1,3,2,0:T(8,128)S(1)} %fusion.111, pred[]{:T(512)S(6)} %compare.7, f32[16,4,256,64]{2,3,1,0:T(8,128)S(1)} %bitcast.187, s32[16]{0:T(128)S(1)} %get-tuple-element.319), kind=kOutput, calls=%fused_computation.45.clone.1 | convolution fusion | flops 408945152 | bytes 29360192 | tf_op jit(solution)/shard_map/while/body/eval_jaxpr/ps,pran->rasn/dot_general | solution.py:67
  84.0 9.1 %fusion.111 = f32[4,256,64,32]{1,3,2,0:T(8,128)S(1)} fusion(f32[16,4,256,64]{2,3,1,0:T(8,128)S(1)} %convolution_bitcast_fusion.5, f32[16]{0:T(128)S(1)} %fusion.110, s32[16]{0:T(128)S(1)} %get-tuple-element.316), kind=kOutput, calls=%fused_computation.46.clone.1 | convolution fusion | flops 402654208 | bytes 12583040 | tf_op jit(solution)/shard_map/while/body/eval_jaxpr/ps,pram->rasm/dot_general | solution.py:70
  93.2 10.6 %bitcast_add_fusion.5 = f32[4,256,32,64]{1,2,3,0:T(8,128)} fusion(f32[4,256,32,64]{1,2,3,0:T(8,128)} %get-tuple-element.328, f32[4,256,64,32]{1,3,2,0:T(8,128)S(1)} %fusion.111, pred[]{:T(512)S(6)} %compare.7, f32[16,4,256,64]{2,3,1,0:T(8,128)S(1)} %bitcast.187, s32[16]{0:T(128)S(1)} %get-tuple-element.319), kind=kOutput, calls=%fused_computation.45.clone.1 | convolution fusion | flops 408945152 | bytes 29360192 | tf_op jit(solution)/shard_map/while/body/eval_jaxpr/ps,pran->rasn/dot_general | solution.py:67
  117.6 4.0 %convert_element_type.64 = bf16[4,256,32,64]{1,2,3,0:T(8,128)(2,1)S(1)} convert(f32[4,256,32,64]{1,2,3,0:T(8,128)} %get-tuple-element.77) | non-fusion elementwise | flops 2097152 | bytes 12582912 | tf_op jit(solution)/shard_map/convert_element_type | solution.py:77
  121.6 3.2 %copy.35 = bf16[4,256,32,64]{1,0,3,2:T(4,128)(2,1)S(1)} copy(bf16[4,256,32,64]{1,2,3,0:T(8,128)(2,1)S(1)} %convert_element_type.64) | data formatting | bytes 8388608 | tf_op jit(solution)/shard_map/convert_element_type | solution.py:77
  124.9 3.1 %copy.47 = bf16[256,8,4,256]{3,1,2,0:T(8,128)(2,1)} copy(bf16[256,8,4,256]{3,2,1,0:T(4,128)(2,1)S(1)} %bitcast.192) | data formatting | bytes 8388608
  127.9 4.4 %reshape_squeeze.6 = bf16[2,16,4,64,64]{4,3,2,1,0:T(8,128)(2,1)} reshape(bf16[1,1,32,4,4096]{4,3,1,0,2:T(4,128)(2,1)} %all-gather.8.cloned.1.call-done) | data formatting | bytes 2097152 | tf_op jit(solution)/shard_map/reshape;squeeze | solution.py:47
  132.3 51.8 %while.24 = (s32[]{:T(128)}, f32[4,256,32,64]{1,2,3,0:T(8,128)}, s32[2,16,2]{1,2,0:T(2,128)S(1)}, bf16[32,64,256]{2,1,0:T(8,128)(2,1)S(1)}, bf16[2,16,4,64,64]{4,3,2,1,0:T(8,128)(2,1)}, /*index=5*/s32[]{:T(128)}, s32[]{:T(128)}) while((s32[]{:T(128)}, f32[4,256,32,64]{1,2,3,0:T(8,128)}, s32[2,16,2]{1,2,0:T(2,128)S(1)}, ...), condition=%wide.region_1.3_spmd.clone.clone, body=%wide.region_0.2_spmd.clone.clone.sunk | while | flops 1080561408 | bytes 58730048 | solution.py:76
  139.7 9.1 %fusion.100 = f32[4,256,64,32]{1,3,2,0:T(8,128)S(1)} fusion(f32[16,4,256,64]{2,3,1,0:T(8,128)S(1)} %convolution_bitcast_fusion.4, f32[16]{0:T(128)S(1)} %fusion.99, s32[16]{0:T(128)S(1)} %get-tuple-element.303), kind=kOutput, calls=%fused_computation.7.clone.1 | convolution fusion | flops 402654208 | bytes 12583040 | tf_op jit(solution)/shard_map/while/body/eval_jaxpr/ps,pram->rasm/dot_general | solution.py:70
  148.9 8.1 %bitcast_add_fusion.4 = f32[4,256,32,64]{1,2,3,0:T(8,128)} fusion(f32[4,256,32,64]{1,2,3,0:T(8,128)} %get-tuple-element.349, f32[4,256,64,32]{1,3,2,0:T(8,128)S(1)} %fusion.100, pred[]{:T(512)S(6)} %compare.6, f32[16,4,256,64]{2,3,1,0:T(8,128)S(1)} %bitcast.188, s32[16]{0:T(128)S(1)} %get-tuple-element.306), kind=kOutput, calls=%fused_computation.6.clone.1 | convolution fusion | flops 408945152 | bytes 29360192 | tf_op jit(solution)/shard_map/while/body/eval_jaxpr/ps,pran->rasn/dot_general | solution.py:67
  164.4 9.1 %fusion.100 = f32[4,256,64,32]{1,3,2,0:T(8,128)S(1)} fusion(f32[16,4,256,64]{2,3,1,0:T(8,128)S(1)} %convolution_bitcast_fusion.4, f32[16]{0:T(128)S(1)} %fusion.99, s32[16]{0:T(128)S(1)} %get-tuple-element.303), kind=kOutput, calls=%fused_computation.7.clone.1 | convolution fusion | flops 402654208 | bytes 12583040 | tf_op jit(solution)/shard_map/while/body/eval_jaxpr/ps,pram->rasm/dot_general | solution.py:70
  173.6 10.3 %bitcast_add_fusion.4 = f32[4,256,32,64]{1,2,3,0:T(8,128)} fusion(f32[4,256,32,64]{1,2,3,0:T(8,128)} %get-tuple-element.349, f32[4,256,64,32]{1,3,2,0:T(8,128)S(1)} %fusion.100, pred[]{:T(512)S(6)} %compare.6, f32[16,4,256,64]{2,3,1,0:T(8,128)S(1)} %bitcast.188, s32[16]{0:T(128)S(1)} %get-tuple-element.306), kind=kOutput, calls=%fused_computation.6.clone.1 | convolution fusion | flops 408945152 | bytes 29360192 | tf_op jit(solution)/shard_map/while/body/eval_jaxpr/ps,pran->rasn/dot_general | solution.py:67
  184.1 4.0 %convert_element_type.59 = bf16[4,256,32,64]{1,2,3,0:T(8,128)(2,1)S(1)} convert(f32[4,256,32,64]{1,2,3,0:T(8,128)} %get-tuple-element.76) | non-fusion elementwise | flops 2097152 | bytes 12582912 | tf_op jit(solution)/shard_map/convert_element_type | solution.py:77
  188.1 3.2 %copy.30 = bf16[4,256,32,64]{1,0,3,2:T(4,128)(2,1)S(1)} copy(bf16[4,256,32,64]{1,2,3,0:T(8,128)(2,1)S(1)} %convert_element_type.59) | data formatting | bytes 8388608 | tf_op jit(solution)/shard_map/convert_element_type | solution.py:77
  191.4 3.0 %copy.46 = bf16[256,8,4,256]{3,1,2,0:T(8,128)(2,1)} copy(bf16[256,8,4,256]{3,2,1,0:T(4,128)(2,1)S(1)} %bitcast.193) | data formatting | bytes 8388608
  194.4 12.8 %convolution_convert_fusion.2 = bf16[1024,2048]{1,0:T(8,128)(2,1)S(1)} fusion(bf16[1024,2048]{0,1:T(8,128)(2,1)} %bitcast.194, bf16[2048,2048]{1,0:T(8,128)(2,1)} %all-gather.6.cloned.1.call-done), kind=kOutput, calls=%fused_computation.87 | convolution fusion | flops 8592031744 | bytes 16777216 | tf_op jit(solution)/shard_map/dot_general | solution.py:78
  207.2 11.3 %convolution_convert_fusion.3 = bf16[1024,2048]{1,0:T(8,128)(2,1)} fusion(bf16[1024,2048]{0,1:T(8,128)(2,1)S(1)} %bitcast.195, bf16[2048,2048]{1,0:T(8,128)(2,1)S(1)} %copy-done.7), kind=kOutput, calls=%fused_computation.88 | convolution fusion | flops 8592031744 | bytes 16777216 | tf_op jit(solution)/shard_map/dot_general | solution.py:78
  218.5 6.5 %pad_maximum_fusion = bf16[2,1,4,256,2048]{4,3,2,1,0:T(8,128)(2,1)} fusion(bf16[1,1,4,256,2048]{4,3,2,1,0:T(8,128)(2,1)S(1)} %bitcast.196, bf16[1,1,4,256,2048]{4,3,2,1,0:T(8,128)(2,1)} %bitcast.197), kind=kLoop, calls=%fused_computation.84 | loop fusion | flops 4194304 | bytes 16777216 | tf_op jit(solution)/shard_map/stack | solution.py:86
  (90 shorter events, 35.6 us)
Async XLA Ops:
  6.5 4.7 %copy-start = (bf16[1,4096,256]{2,1,0:T(8,128)(2,1)S(1)}, bf16[1,4096,256]{2,1,0:T(8,128)(2,1)}, u32[]{:S(2)}) copy-start(bf16[1,4096,256]{2,1,0:T(8,128)(2,1)} %param.12) | copy-start | bytes 6291460
  6.5 28.5 %copy-start.6 = (s32[32,2]{0,1:T(2,128)S(1)}, s32[32,2]{0,1:T(2,128)}, u32[]{:S(2)}) copy-start(s32[32,2]{0,1:T(2,128)} %param.13) | copy-start | bytes 772
  6.5 40.6 %all-gather.10.cloned.1.call-start = ((), (), s32[]{:S(2)}) async-start(), calls=%async_computation.4 | async-start | bytes 1179648 | tf_op jit(solution)/shard_map/all_gather | solution.py:26
  11.9 39.6 %copy-start.2 = (bf16[2048,256]{1,0:T(8,128)(2,1)S(1)}, bf16[2048,256]{1,0:T(8,128)(2,1)}, u32[]{:S(2)}) copy-start(bf16[2048,256]{1,0:T(8,128)(2,1)} %param.16) | copy-start | bytes 3145732
  24.4 103.5 %all-gather.8.cloned.1.call-start = ((), (), s32[]{:S(2)}) async-start(), calls=%async_computation.3 | async-start | bytes 1179648 | tf_op jit(solution)/shard_map/all_gather | solution.py:26
  34.3 160.1 %all-gather.6.cloned.1.call-start = ((), (), s32[]{:S(2)}) async-start(), calls=%async_computation.2 | async-start | bytes 9437184 | tf_op jit(solution)/shard_map/all_gather | solution.py:80
  56.6 1.9 copy-start.3
  81.3 2.0 copy-start.3
  137.1 1.9 copy-start.4
  161.8 1.9 copy-start.4
  194.4 12.8 %copy-start.5 = (bf16[256,8,4,256]{3,1,2,0:T(8,128)(2,1)S(1)}, bf16[256,8,4,256]{3,1,2,0:T(8,128)(2,1)}, u32[]{:S(2)}) copy-start(bf16[256,8,4,256]{3,1,2,0:T(8,128)(2,1)} %copy.46) | copy-start | bytes 12582916
  194.4 12.8 %copy-start.7 = (bf16[2048,2048]{1,0:T(8,128)(2,1)S(1)}, bf16[2048,2048]{1,0:T(8,128)(2,1)}, u32[]{:S(2)}) copy-start(bf16[2048,2048]{1,0:T(8,128)(2,1)} %all-gather.6.cloned.1.call-done) | copy-start | bytes 25165828
  218.5 6.5 %copy-start.1 = (bf16[1,4096,256]{2,1,0:T(8,128)(2,1)S(1)}, bf16[1,4096,256]{2,1,0:T(8,128)(2,1)}, u32[]{:S(2)}) copy-start(bf16[1,4096,256]{2,1,0:T(8,128)(2,1)} %param.12) | copy-start | bytes 6291460
Sparse Core Ops, SparseCore 0:
  24.6 22.5 all-gather.9
  49.1 23.4 all-gather.7
  74.5 55.9 all-gather.5
where the time goes:
time: 235 us; the launch traced here: 232 us
  matrix products  110 us (47%)
  local copies, waits for them, and re-layouts  42.5 us (18%)
  blocking collectives  21.4 us (9%)
  other arithmetic  16.3 us (7%)
  between operations  15 us (6%)
  loops' own time  14.5 us (6%)
  waiting for transfers between devices  12.6 us (5%)
    dot_general x4, matrix products, accumulate(): jnp.einsum('ps,pran->rasn', place_two, term_one, precision=lax.Precision....  37.2 us
    dot_general x4, matrix products, accumulate(): jnp.einsum('ps,pram->rasm', place_one, term_two, precision=lax.Precision....  36.6 us
    dot_general x2, matrix products, bra_transform(): jnp.dot(left_rounded, lax.all_gather(coef_act, 'mo', axis=1, tiled=True),...  24.1 us
    all_to_all x2, blocking collectives, remap_pairs(): lax.all_to_all(stacked, 'ao', split_axis=2, concat_axis=1, tiled=True)  21.4 us
    another operation x2, loops' own time, bra_transform(): left_terms = lax.scan(accumulate, start_terms, (grouped, grouped_pairs))[0]  14.5 us
    all_gather x2, waiting for transfers between devices, remap_pairs(): return lax.all_gather(owned, 'mo', axis=1, tiled=True)  11.8 us
    another operation x2, local copies, waits for them, and re-layouts, bra_transform(): grouped = gathered.reshape(block_count // 16, 16, pair_rows, SH, SH)  8.71 us
    convert_element_type x2, other arithmetic, bra_transform(): left_terms.astype(jnp.bfloat16).reshape(pair_rows * panel_width, ao_width)  8.08 us
  transfers between devices with their start and end apart: 3, of which 1 were waited for; matrix products, arithmetic and copies ran while one was open for 58% of the time, Pallas kernels for 0%

commit v1 on v0

v1 whole, which is shorter than its diff:
```python
import functools

import jax
import jax.numpy as jnp
from jax import lax
from jax.experimental import pallas as pl
from jax.experimental.pallas import tpu as pltpu
from jax.sharding import PartitionSpec as P

SH = 64
NSH = 32
ACT = 2048
KL = 16
KS = 16
NI = 4
MESH = pl.DeviceIdType.MESH


def pair_coefficients(occ_lam, occ_sig, slab_index):
    nj_all = occ_sig.shape[1]
    lam_cols = lax.dynamic_slice_in_dim(occ_lam, slab_index * NI, NI, 1).astype(jnp.float32)
    pair_coef = occ_sig.astype(jnp.float32).T[:, None, None, :] * lam_cols.T[None, :, :, None]
    return pair_coef.reshape(nj_all, NI, KL * KS).astype(jnp.bfloat16)


def term_order(shell_pairs, slot):
    one, two = shell_pairs[:, 0], shell_pairs[:, 1]
    count = 2 * one.shape[0]
    target = jnp.concatenate([two, jnp.where(one != two, one, NSH)])
    source = jnp.concatenate([one, two])
    block = jnp.concatenate([slot, slot + one.shape[0]])
    key = target * count + jnp.arange(count, dtype=jnp.int32)
    rank = jnp.sum((key[None, :] < key[:, None]).astype(jnp.int32), axis=1)
    here = (rank[None, :] == jnp.arange(count, dtype=jnp.int32)[:, None]).astype(jnp.int32)
    keep = jnp.sum(jnp.where((target[None, :] == target[:, None]) & (key[None, :] < key[:, None]), 1, 0), axis=1)
    keep = (keep > 0).astype(jnp.int32)
    terms = jnp.stack([source, block, keep])
    terms = jnp.sum(here[None] * terms[:, None, :], axis=2)
    shells = jnp.arange(NSH, dtype=jnp.int32)
    upto = jnp.sum((target[None, :] <= shells[:, None]).astype(jnp.int32), axis=1)
    has = jnp.sum((target[None, :] == shells[:, None]).astype(jnp.int32), axis=1)
    return terms, jnp.stack([jnp.maximum(upto - 1, 0), (has > 0).astype(jnp.int32)])


def fused_kernel(
    terms, last, half, coef, out,
    hbuf, cbuf, carry, sums, left, stage,
    hz_send, hz_recv, h_send, h_recv, c_send, c_recv, o_sem,
):
    z = lax.axis_index("ao")
    me = lax.axis_index("mo")

    def flip(step):
        return me + step * (1 - 2 * lax.rem(me // step, 2))

    sibling = flip(1)
    across_x = flip(2)
    across_y = flip(4)
    across_d = across_x + across_y - me
    barrier = pltpu.get_barrier_semaphore()
    for peer in (sibling, across_x, across_y, across_d):
        pl.semaphore_signal(barrier, inc=1, device_id={"mo": peer}, device_id_type=MESH)
    for d in range(1, 4):
        pl.semaphore_signal(barrier, inc=1, device_id={"ao": lax.rem(z + d, 4)}, device_id_type=MESH)
    pl.semaphore_wait(barrier, 7)

    def send(src, dst, send_sem, recv_sem, device):
        copy = pltpu.make_async_remote_copy(
            src_ref=src, dst_ref=dst, send_sem=send_sem, recv_sem=recv_sem,
            device_id=device, device_id_type=MESH,
        )
        copy.start()
        return copy

    shells_half = NSH // 2
    low, high = pl.ds(0, shells_half), pl.ds(shells_half, shells_half)

    def send_coef(src, slot, part, index, peer):
        return send(src, cbuf.at[slot, part], c_send.at[index], c_recv.at[index], {"mo": peer})

    c_copies = {}
    z_copies = [
        send(half.at[lax.rem(z + d, 4)], hbuf.at[z], hz_send.at[d - 1], hz_recv.at[d - 1], {"ao": lax.rem(z + d, 4)})
        for d in range(1, 4)
    ]
    c_copies["xh"] = send_coef(coef.at[high], 2, high, 0, across_x)
    c_copies["yl"] = send_coef(coef.at[low], 4, low, 1, across_y)
    hbuf[z] = half[z]
    for copy in z_copies:
        copy.wait()

    def send_half(src_slot, dst_slot, index, peer):
        return send(
            hbuf.at[pl.ds(4 * src_slot, 4)], hbuf.at[pl.ds(4 * dst_slot, 4)],
            h_send.at[index], h_recv.at[index], {"mo": peer},
        )

    h_d = send_half(0, 6, 5, across_d)
    h_x = send_half(0, 2, 1, across_x)
    h_y = send_half(0, 4, 3, across_y)
    h_s = send_half(0, 1, 0, sibling)
    c_copies["xl"] = send_coef(coef.at[low], 2, low, 2, across_x)
    c_copies["yh"] = send_coef(coef.at[high], 4, high, 3, across_y)
    c_copies["s"] = send_coef(coef, 1, pl.ds(0, NSH), 4, sibling)
    h_x.wait_recv()
    h_sx = send_half(2, 3, 2, sibling)
    h_y.wait_recv()
    h_sy = send_half(4, 5, 4, sibling)
    h_d.wait_recv()
    h_sd = send_half(6, 7, 6, sibling)
    c_copies["xh"].wait_recv()
    c_copies["dh"] = send_coef(cbuf.at[2, high], 6, high, 5, across_y)
    c_copies["yl"].wait_recv()
    c_copies["dl"] = send_coef(cbuf.at[4, low], 6, low, 6, across_x)
    for copy in (h_s, h_sx, h_sy, h_sd):
        copy.wait()
    for copy in (h_x, h_y, h_d):
        copy.wait_send()

    blocks = 32
    rows = 8

    def turn(block, _):
        values = hbuf[block].astype(jnp.float32).T
        turned = jnp.concatenate([values[r * SH:(r + 1) * SH, :] for r in range(rows)], axis=1)
        hbuf[block + blocks] = turned.astype(jnp.bfloat16)
        return 0

    lax.fori_loop(0, blocks, turn, 0)
    carry[...] = jnp.zeros_like(carry)

    def add_term(t, _):
        added = lax.dot_general(
            coef[terms[0, t]], hbuf[terms[1, t]], (((0,), (0,)), ((), ())), preferred_element_type=jnp.float32
        )
        total = jnp.where(terms[2, t] > 0, carry[...], 0.0) + added
        carry[...] = total
        sums[t] = total.astype(jnp.bfloat16)
        return 0

    lax.fori_loop(0, 2 * blocks, add_term, 0)

    c_copies["xl"].wait_recv()
    c_copies["sx"] = send_coef(cbuf.at[2], 3, pl.ds(0, NSH), 7, sibling)
    c_copies["yh"].wait_recv()
    c_copies["sy"] = send_coef(cbuf.at[4], 5, pl.ds(0, NSH), 8, sibling)

    width = coef.shape[2]

    def place(u, _):
        zero = jnp.zeros((width, rows * SH), jnp.bfloat16)
        first = jnp.where(last[1, 2 * u] > 0, sums[last[0, 2 * u]], zero)
        second = jnp.where(last[1, 2 * u + 1] > 0, sums[last[0, 2 * u + 1]], zero)
        columns = pl.ds(pl.multiple_of(u * 2 * SH, 2 * SH), 2 * SH)
        for r in range(rows):
            both = jnp.concatenate([first[:, r * SH:(r + 1) * SH], second[:, r * SH:(r + 1) * SH]], axis=1)
            left[r * width:(r + 1) * width, columns] = both
        return 0

    lax.fori_loop(0, NSH // 2, place, 0)

    out_copies = [None, None]
    height = 2 * width

    def panel(step, slot):
        buf = step % 2
        if out_copies[buf] is not None:
            out_copies[buf].wait()
        ref = coef if slot == 0 else cbuf.at[slot]

        def tile(m, _):
            part = jnp.dot(
                left[pl.ds(pl.multiple_of(m * height, height), height), :],
                ref[...].reshape(NSH * SH, width),
                preferred_element_type=jnp.float32,
            ).astype(jnp.bfloat16)
            stage[buf, pl.ds(m * 2, 2)] = part.reshape(2, width, width)
            return 0

        lax.fori_loop(0, rows // 2, tile, 0)
        source = me
        for bit in (1, 2, 4):
            if slot & bit:
                source = source + flip(bit) - me
        columns = pl.ds(pl.multiple_of(source * width, width), width)
        copy = pltpu.make_async_copy(stage.at[buf], out.at[:, :, columns], o_sem.at[buf])
        copy.start()
        out_copies[buf] = copy

    panel(0, 0)
    c_copies["s"].wait_recv()
    panel(1, 1)
    panel(2, 2)
    c_copies["dh"].wait_recv()
    c_copies["dl"].wait_recv()
    c_copies["sd"] = send_coef(cbuf.at[6], 7, pl.ds(0, NSH), 9, sibling)
    panel(3, 4)
    c_copies["sx"].wait_recv()
    panel(4, 3)
    c_copies["sy"].wait_recv()
    panel(5, 5)
    panel(6, 6)
    c_copies["sd"].wait_recv()
    panel(7, 7)
    for copy in c_copies.values():
        copy.wait_send()
    for copy in out_copies:
        copy.wait()


def fused_body(pair_ints, shell_pairs, occ_lam, occ_sig, coef_act, slabs):
    width = coef_act.shape[1]
    blocks = shell_pairs.shape[0]
    me = lax.axis_index("mo").astype(jnp.int32)
    number = jnp.arange(blocks, dtype=jnp.int32)
    slot = jnp.bitwise_xor(number % 8, me) * 4 + number // 8
    terms, last = term_order(shell_pairs, slot)
    pair_coef = jnp.stack([pair_coefficients(occ_lam, occ_sig, slabs[k]) for k in range(2)], axis=1)
    rows = 2 * NI
    half = jnp.einsum(
        "mnw,jrw->jmrn", pair_ints.reshape(SH, SH, KL * KS), pair_coef.reshape(4, rows, KL * KS),
        preferred_element_type=jnp.float32,
    ).astype(jnp.bfloat16).reshape(4, SH, rows * SH)
    coef = coef_act.reshape(NSH, SH, width)
    dma = pltpu.SemaphoreType.DMA
    vmem = pl.BlockSpec(memory_space=pltpu.VMEM)
    smem = pl.BlockSpec(memory_space=pltpu.SMEM)
    result = pl.pallas_call(
        fused_kernel,
        out_shape=jax.ShapeDtypeStruct((rows, width, ACT), jnp.bfloat16),
        in_specs=[smem, smem, vmem, vmem],
        out_specs=pl.BlockSpec(memory_space=pl.ANY),
        scratch_shapes=[
            pltpu.VMEM((2 * blocks, SH, rows * SH), jnp.bfloat16),
            pltpu.VMEM((8, NSH, SH, width), jnp.bfloat16),
            pltpu.VMEM((width, rows * SH), jnp.float32),
            pltpu.VMEM((2 * blocks, width, rows * SH), jnp.bfloat16),
            pltpu.VMEM((rows * width, NSH * SH), jnp.bfloat16),
            pltpu.VMEM((2, rows, width, width), jnp.bfloat16),
            dma((3,)), dma((3,)), dma((7,)), dma((7,)), dma((10,)), dma((10,)), dma((2,)),
        ],
        compiler_params=pltpu.CompilerParams(
            collective_id=0, has_side_effects=True, vmem_limit_bytes=56 * 2 ** 20
        ),
        cost_estimate=pl.CostEstimate(
            flops=2 * rows * width * ACT * ACT, bytes_accessed=12 * 2 ** 20, transcendentals=0
        ),
    )(terms, last, half, coef)
    return result.reshape(2, 1, NI, width, ACT)


def ket_transform(pair_ints, occ_lam, occ_sig, slab_index):
    blocks_here = pair_ints.shape[0]
    nj_all = occ_sig.shape[1]
    pair_coef = pair_coefficients(occ_lam, occ_sig, slab_index).reshape(nj_all * NI, KL * KS)
    half_ints = jnp.einsum("bqw,xw->bxq", pair_ints, pair_coef, preferred_element_type=jnp.float32)
    return half_ints.astype(jnp.bfloat16).reshape(blocks_here, nj_all, NI, SH * SH)


def remap_pairs(stacked):
    owned = lax.all_to_all(stacked, "ao", split_axis=2, concat_axis=1, tiled=True)
    return lax.all_gather(owned, "mo", axis=1, tiled=True)


def general_body(pair_ints, shell_pairs, occ_lam, occ_sig, coef_act, slabs):
    ao_count = lax.axis_size("ao")
    mo_count = lax.axis_size("mo")
    blocks_here = pair_ints.shape[0]
    panel_width = coef_act.shape[1]
    ao_width = coef_act.shape[0]
    ordered_pairs = (
        shell_pairs.reshape(ao_count, mo_count, blocks_here, 2).transpose(1, 0, 2, 3).reshape(-1, 2)
    )
    halves = [ket_transform(pair_ints, occ_lam, occ_sig, slabs[k]) for k in range(2)]
    gathered_slabs = [remap_pairs(single[None])[0] for single in halves]
    coef_shells = coef_act.reshape(NSH, SH, panel_width)
    coef_all = lax.all_gather(coef_act, "mo", axis=1, tiled=True)

    def bra_transform(gathered):
        block_count = gathered.shape[0]
        pair_rows = gathered.shape[1] * gathered.shape[2]
        blocks = gathered.reshape(block_count, pair_rows, SH, SH)

        def accumulate(running, item):
            values, pair = item
            term_one = jnp.einsum(
                "rmn,ma->ran", values, coef_shells[pair[0]], preferred_element_type=jnp.float32
            )
            term_two = jnp.einsum(
                "rmn,na->ram", values, coef_shells[pair[1]], preferred_element_type=jnp.float32
            ) * (pair[0] != pair[1]).astype(jnp.float32)
            running = running.at[pair[1]].add(term_one)
            return running.at[pair[0]].add(term_two), None

        start_terms = jnp.zeros((NSH, pair_rows, panel_width, SH), jnp.float32)
        left_terms = lax.scan(accumulate, start_terms, (blocks, ordered_pairs))[0]
        left_rounded = left_terms.astype(jnp.bfloat16).transpose(1, 2, 0, 3)
        product = jnp.dot(
            left_rounded.reshape(pair_rows * panel_width, ao_width), coef_all, preferred_element_type=jnp.float32
        )
        return product.astype(jnp.bfloat16).reshape(gathered.shape[1], NI, panel_width, ACT)

    return jnp.stack([bra_transform(gathered) for gathered in gathered_slabs])


def solution(mesh):
    fits = mesh.shape["ao"] == 4 and mesh.shape["mo"] == 8
    return jax.shard_map(
        fused_body if fits else general_body,
        mesh=mesh,
        in_specs=(P(("ao", "mo"), None, None), P(), P(), P(), P(None, "mo"), P()),
        out_specs=P(None, "ao", None, "mo", None),
        check_vma=False,
    )
```

time: 235 us -> 105 us (0.45); the launches traced: 232 us -> 105 us
  matrix products: 110 us -> 1.05 us
  Pallas kernels: 0 us -> 84.7 us
  local copies, waits for them, and re-layouts: 42.5 us -> 13 us
  blocking collectives: 21.4 us -> 0 us
  loops' own time: 14.5 us -> 0 us
  between operations: 15 us -> 1.43 us
  waiting for transfers between devices: 12.6 us -> 0 us
  other arithmetic: 16.3 us -> 4.81 us
    dot_general x16 -> x1, matrix products: 102 us -> 1.05 us  [fused_body(): jnp.einsum('mnw,jrw->jmrn', pair_ints.reshape(SH, SH, KL * KS), pair_coef...]
    pallas_call x0 -> x1, Pallas kernels: none -> 84.7 us  [fused_body(): pl.pallas_call(fused_kernel, out_shape=jax.ShapeDtypeStruct((rows, width,...]
    all_to_all x2 -> x0, blocking collectives: 21.4 us -> none  [remap_pairs(): lax.all_to_all(stacked, 'ao', split_axis=2, concat_axis=1, tiled=True)]
    another operation x2 -> x0, loops' own time: 14.5 us -> none  [bra_transform(): left_terms = lax.scan(accumulate, start_terms, (grouped, grouped_pairs))[0]]
    all_gather x3 -> x0, waiting for transfers between devices: 11.8 us -> none  [the longest x2 11.8 us: remap_pairs(): return lax.all_gather(owned, 'mo', axis=1, tiled=True)]
    gather x8 -> x0, local copies, waits for them, and re-layouts: 11 us -> none  [the longest x4 5.52 us: accumulate(): coef_two = jnp.take(coef_shells, shell_two, axis=0)]
    another operation x5 -> x0, local copies, waits for them, and re-layouts: 8.94 us -> none  [the longest x2 8.71 us: bra_transform(): grouped = gathered.reshape(block_count // 16, 16, pair_rows, SH, SH)]
    convert_element_type x3 -> x4, other arithmetic: 8.17 us -> 0.03 us  [the longest x1 0.01 us: pair_coefficients(): return pair_coef.reshape(nj_all, NI, KL * KS).astype(jnp.bfloat16)]
  transfers between devices with their start and end apart: 3 -> 0, of which waited for: 1 -> 0; matrix products, arithmetic and copies ran while one was open for 58% -> 0% of each run, Pallas kernels for 0% -> 0%
where the time goes in v1:
time: 105 us
  Pallas kernels  84.7 us (81%)
  local copies, waits for them, and re-layouts  13 us (12%)
  other arithmetic  4.81 us (5%)
  between operations  1.43 us (1%)
  matrix products  1.05 us (1%)
    pallas_call x1, Pallas kernels, fused_body(): pl.pallas_call(fused_kernel, out_shape=jax.ShapeDtypeStruct((rows, width,...  84.7 us
    unnamed x3, local copies, waits for them, and re-layouts  10 us

profile of v1, /device:TPU:0, one launch (start us, length us, event | category | flops | bytes accessed | tf_op | source)
XLA Modules:
  0.0 105.0 jit_solution(11582899011626514946)
XLA Ops:
  0.0 0.0 copy-start
  0.0 1.6 %copy-done = bf16[1,4096,256]{2,1,0:T(8,128)(2,1)S(1)} copy-done((bf16[1,4096,256]{2,1,0:T(8,128)(2,1)S(1)}, bf16[1,4096,256]{2,1,0:T(8,128)(2,1)}, u32[]{:S(2)}) %copy-start) | copy-done | bytes 2097176
  1.6 0.8 compare_select_fusion.1
  2.4 0.1 add_bitcast_fusion.1
  2.4 1.4 %fusion.11 = (s32[1]{0:T(128)}, s32[1]{0:T(128)}) fusion(s32[2]{0:T(128)} %param.11), kind=kLoop, calls=%fused_computation.46 | loop fusion | bytes 16 | tf_op jit(solution)/shard_map/slice | solution.py:218
  5.2 0.8 slice_bitcast_fusion
  5.9 0.1 iota_add_fusion
  6.0 0.2 fusion.1
  6.2 0.1 convert_reduce_fusion.1
  6.4 0.5 pad_add_fusion.1.last
  6.9 0.7 convert_bitcast_fusion.2
  7.6 0.8 convert_bitcast_fusion.1
  8.4 0.1 copy.10
  8.5 0.1 copy.11
  8.6 0.1 mul.118
  8.7 0.1 mul.119
  8.7 0.1 mul.112
  8.8 0.1 mul.113
  8.9 0.1 mul.108
  9.1 0.7 multiply_reduce_fusion.terms
  9.8 1.1 fusion
  10.9 1.0 reshape.149.half
  11.9 84.7 %shard_map.64 = bf16[8,256,2048]{2,1,0:T(8,128)(2,1)} custom-call(s32[3,64]{1,0:T(4,128)} %multiply_reduce_fusion.terms, s32[2,32]{1,0:T(2,128)} %pad_add_fusion.1.last, bf16[4,64,512]{2,1,0:T(8,128)(2,1)} %reshape.149.half, bf16[32,64,256]{2,1,0:T(8,128)(2,1)} %bitcast.45), custom_call_target="tpu_custom_call" | custom-call | flops 17179869184 | bytes 12582912 | tf_op jit(solution)/shard_map/pallas_call | solution.py:228
  96.6 8.4 %copy.15 = bf16[2,1,4,256,2048]{4,3,2,1,0:T(8,128)(2,1)} copy(bf16[2,1,4,256,2048]{4,3,2,1,0:T(8,128)(2,1)} %bitcast.44) | data formatting | bytes 16777216
  (10 shorter events, 0.1 us)
Async XLA Ops:
  0.0 1.6 %copy-start = (bf16[1,4096,256]{2,1,0:T(8,128)(2,1)S(1)}, bf16[1,4096,256]{2,1,0:T(8,128)(2,1)}, u32[]{:S(2)}) copy-start(bf16[1,4096,256]{2,1,0:T(8,128)(2,1)} %param.6) | copy-start | bytes 6291460

commit v2 on v1

--- a/solution.py
+++ b/solution.py
@@ -14,6 +14,8 @@
 KS = 16
 NI = 4
 MESH = pl.DeviceIdType.MESH
+FIRST = (0, 1, 2, 4)
+SECOND = (3, 5, 6, 7)
 
 
 def pair_coefficients(occ_lam, occ_sig, slab_index):
@@ -23,29 +25,101 @@
     return pair_coef.reshape(nj_all, NI, KL * KS).astype(jnp.bfloat16)
 
 
-def term_order(shell_pairs, slot):
-    one, two = shell_pairs[:, 0], shell_pairs[:, 1]
-    count = 2 * one.shape[0]
-    target = jnp.concatenate([two, jnp.where(one != two, one, NSH)])
-    source = jnp.concatenate([one, two])
-    block = jnp.concatenate([slot, slot + one.shape[0]])
-    key = target * count + jnp.arange(count, dtype=jnp.int32)
-    rank = jnp.sum((key[None, :] < key[:, None]).astype(jnp.int32), axis=1)
-    here = (rank[None, :] == jnp.arange(count, dtype=jnp.int32)[:, None]).astype(jnp.int32)
-    keep = jnp.sum(jnp.where((target[None, :] == target[:, None]) & (key[None, :] < key[:, None]), 1, 0), axis=1)
-    keep = (keep > 0).astype(jnp.int32)
-    terms = jnp.stack([source, block, keep])
-    terms = jnp.sum(here[None] * terms[:, None, :], axis=2)
-    shells = jnp.arange(NSH, dtype=jnp.int32)
-    upto = jnp.sum((target[None, :] <= shells[:, None]).astype(jnp.int32), axis=1)
-    has = jnp.sum((target[None, :] == shells[:, None]).astype(jnp.int32), axis=1)
-    return terms, jnp.stack([jnp.maximum(upto - 1, 0), (has > 0).astype(jnp.int32)])
+def prepare_kernel(slabs, me, pairs, occ_lam, occ_sig, terms, last, pair_coef):
+    blocks = pairs.shape[0]
+    count = 2 * blocks
+    numbers = pairs[...]
+    one, two = numbers[:, 0:1], numbers[:, 1:2]
+    block = lax.broadcasted_iota(jnp.int32, (blocks, 1), 0)
+    slot = jnp.bitwise_xor(lax.rem(block, 8), jnp.full((blocks, 1), me[0], jnp.int32)) * 4 + block // 8
+    real = jnp.float32
+    target = jnp.concatenate([two, jnp.where(one != two, one, NSH)], axis=0).astype(real)
+    source = jnp.concatenate([one, two], axis=0).astype(real)
+    place = jnp.concatenate([slot, slot + blocks], axis=0).astype(real)
+    down = lax.broadcasted_iota(jnp.int32, (count, count), 0)
+    along = lax.broadcasted_iota(jnp.int32, (count, count), 1)
+    target_down = jnp.broadcast_to(target, (count, count))
+    target_along = jnp.broadcast_to(
+        jnp.sum(jnp.where(down == along, target_down, 0.0), axis=0, keepdims=True), (count, count)
+    )
+    earlier = (target_along < target_down) | ((target_along == target_down) & (along < down))
+    rank = jnp.sum(jnp.where(earlier, 1.0, 0.0), axis=1, keepdims=True)
+    same = jnp.sum(jnp.where((target_along == target_down) & (along < down), 1.0, 0.0), axis=1, keepdims=True)
+    keep = jnp.where(same > 0.0, 1.0, 0.0)
+    here = rank == along.astype(real)
+    for row, column in enumerate((source, place, keep)):
+        terms[row:row + 1, :] = jnp.sum(jnp.where(here, column, 0.0), axis=0, keepdims=True).astype(jnp.int32)
+    shells = lax.broadcasted_iota(jnp.int32, (count, NSH), 1).astype(real)
+    upto = jnp.sum(jnp.where(target <= shells, 1.0, 0.0), axis=0, keepdims=True)
+    has = jnp.sum(jnp.where(target == shells, 1.0, 0.0), axis=0, keepdims=True)
+    last[0:1, :] = jnp.maximum(upto - 1.0, 0.0).astype(jnp.int32)
+    last[1:2, :] = jnp.minimum(has, 1.0).astype(jnp.int32)
+
+    rows, occupied = pair_coef.shape[0], occ_lam.shape[1]
+    nj_all = occ_sig.shape[1]
+    half = jnp.bfloat16
+
+    def pick(chosen, values, spread):
+        some = lax.dot_general(
+            jnp.where(chosen, 1.0, 0.0).astype(half), values, (((1,), (1,)), ((), ())), preferred_element_type=real
+        )
+        return jnp.dot(some.astype(half), jnp.where(spread, 1.0, 0.0).astype(half), preferred_element_type=real)
+
+    row = lax.broadcasted_iota(jnp.int32, (rows, occupied), 0)
+    column = lax.broadcasted_iota(jnp.int32, (rows, occupied), 1)
+    wanted = jnp.where(lax.rem(row // NI, 2) == 0, slabs[0], slabs[1]) * NI + lax.rem(row, NI)
+    row_j = lax.broadcasted_iota(jnp.int32, (rows, nj_all), 0)
+    column_j = lax.broadcasted_iota(jnp.int32, (rows, nj_all), 1)
+    pair = lax.broadcasted_iota(jnp.int32, (KL, KL * KS), 1)
+    single = lax.broadcasted_iota(jnp.int32, (KL, KL * KS), 0)
+    lam = pick(column == wanted, occ_lam[...], pair // KS == single)
+    sig = pick(column_j == row_j // (2 * NI), occ_sig[...], lax.rem(pair, KS) == single)
+    pair_coef[...] = (lam * sig).astype(half)
+
+
+def rest_kernel(me, left, coefs, done, out, lbuf, cbuf, stage, l_sem, c_sem, d_sem, o_sem):
+    width = cbuf.shape[2]
+    rows = done.shape[1]
+    height = 2 * width
+
+    def columns(slot):
+        return pl.ds(pl.multiple_of(jnp.bitwise_xor(me[0], slot) * width, width), width)
+
+    loads = [pltpu.make_async_copy(coefs.at[n], cbuf.at[n], c_sem.at[n]) for n in range(4)]
+    lefts = [
+        pltpu.make_async_copy(left.at[pl.ds(m * height, height)], lbuf.at[m], l_sem.at[m]) for m in range(rows // 2)
+    ]
+    loads[0].start()
+    lefts[0].start()
+    for copy in loads[1:] + lefts[1:]:
+        copy.start()
+    moves = [
+        pltpu.make_async_copy(done.at[n], out.at[:, :, columns(slot)], d_sem.at[n])
+        for n, slot in enumerate(FIRST)
+    ]
+    for copy in moves:
+        copy.start()
+    stores = []
+    for m in range(rows // 2):
+        lefts[m].wait()
+        for n, slot in enumerate(SECOND):
+            if m == 0:
+                loads[n].wait()
+            part = jnp.dot(lbuf[m], cbuf[n], preferred_element_type=jnp.float32).astype(jnp.bfloat16)
+            stage[m, n] = part.reshape(2, width, width)
+            copy = pltpu.make_async_copy(
+                stage.at[m, n], out.at[pl.ds(2 * m, 2), :, columns(slot)], o_sem.at[m, n]
+            )
+            copy.start()
+            stores.append(copy)
+    for copy in moves + stores:
+        copy.wait()
 
 
 def fused_kernel(
-    terms, last, half, coef, out,
+    terms, last, half, coef, left_out, coefs_out, out,
     hbuf, cbuf, carry, sums, left, stage,
-    hz_send, hz_recv, h_send, h_recv, c_send, c_recv, o_sem,
+    hz_send, hz_recv, h_send, h_recv, c_send, c_recv, o_sem, l_sem, k_sem,
 ):
     z = lax.axis_index("ao")
     me = lax.axis_index("mo")
@@ -72,19 +146,31 @@
         copy.start()
         return copy
 
-    shells_half = NSH // 2
-    low, high = pl.ds(0, shells_half), pl.ds(shells_half, shells_half)
+    blocks = 32
+    rows = 8
+    quarter = NSH // 4
+    low, high = pl.ds(0, 2 * quarter), pl.ds(2 * quarter, 2 * quarter)
+    parts = [pl.ds(n * quarter, quarter) for n in range(4)]
 
     def send_coef(src, slot, part, index, peer):
         return send(src, cbuf.at[slot, part], c_send.at[index], c_recv.at[index], {"mo": peer})
+
+    def turn(block, _):
+        values = hbuf[block].astype(jnp.float32).T
+        turned = jnp.concatenate([values[r * SH:(r + 1) * SH, :] for r in range(rows)], axis=1)
+        hbuf[block + blocks] = turned.astype(jnp.bfloat16)
+        return 0
+
+    def turn_slot(slot):
+        lax.fori_loop(4 * slot, 4 * slot + 4, turn, 0)
 
     c_copies = {}
     z_copies = [
         send(half.at[lax.rem(z + d, 4)], hbuf.at[z], hz_send.at[d - 1], hz_recv.at[d - 1], {"ao": lax.rem(z + d, 4)})
         for d in range(1, 4)
     ]
-    c_copies["xh"] = send_coef(coef.at[high], 2, high, 0, across_x)
-    c_copies["yl"] = send_coef(coef.at[low], 4, low, 1, across_y)
+    c_copies["x2"] = send_coef(coef.at[parts[2]], 2, parts[2], 0, across_x)
+    c_copies["y0"] = send_coef(coef.at[parts[0]], 4, parts[0], 1, across_y)
     hbuf[z] = half[z]
     for copy in z_copies:
         copy.wait()
@@ -99,34 +185,31 @@
     h_x = send_half(0, 2, 1, across_x)
     h_y = send_half(0, 4, 3, across_y)
     h_s = send_half(0, 1, 0, sibling)
-    c_copies["xl"] = send_coef(coef.at[low], 2, low, 2, across_x)
-    c_copies["yh"] = send_coef(coef.at[high], 4, high, 3, across_y)
     c_copies["s"] = send_coef(coef, 1, pl.ds(0, NSH), 4, sibling)
+    turn_slot(0)
+    h_s.wait_recv()
+    turn_slot(1)
     h_x.wait_recv()
     h_sx = send_half(2, 3, 2, sibling)
     h_y.wait_recv()
     h_sy = send_half(4, 5, 4, sibling)
+    c_copies["x3"] = send_coef(coef.at[parts[3]], 2, parts[3], 10, across_x)
+    c_copies["y1"] = send_coef(coef.at[parts[1]], 4, parts[1], 11, across_y)
+    c_copies["xl"] = send_coef(coef.at[low], 2, low, 2, across_x)
+    c_copies["yh"] = send_coef(coef.at[high], 4, high, 3, across_y)
+    turn_slot(2)
+    turn_slot(4)
     h_d.wait_recv()
     h_sd = send_half(6, 7, 6, sibling)
-    c_copies["xh"].wait_recv()
-    c_copies["dh"] = send_coef(cbuf.at[2, high], 6, high, 5, across_y)
-    c_copies["yl"].wait_recv()
-    c_copies["dl"] = send_coef(cbuf.at[4, low], 6, low, 6, across_x)
-    for copy in (h_s, h_sx, h_sy, h_sd):
-        copy.wait()
-    for copy in (h_x, h_y, h_d):
+    h_sx.wait_recv()
+    turn_slot(3)
+    h_sy.wait_recv()
+    turn_slot(5)
+    turn_slot(6)
+    h_sd.wait_recv()
+    turn_slot(7)
+    for copy in (h_s, h_x, h_y, h_d, h_sx, h_sy, h_sd):
         copy.wait_send()
-
-    blocks = 32
-    rows = 8
-
-    def turn(block, _):
-        values = hbuf[block].astype(jnp.float32).T
-        turned = jnp.concatenate([values[r * SH:(r + 1) * SH, :] for r in range(rows)], axis=1)
-        hbuf[block + blocks] = turned.astype(jnp.bfloat16)
-        return 0
-
-    lax.fori_loop(0, blocks, turn, 0)
     carry[...] = jnp.zeros_like(carry)
 
     def add_term(t, _):
@@ -138,7 +221,14 @@
         sums[t] = total.astype(jnp.bfloat16)
         return 0
 
-    lax.fori_loop(0, 2 * blocks, add_term, 0)
+    lax.fori_loop(0, blocks, add_term, 0)
+    c_copies["x2"].wait_recv()
+    c_copies["x3"].wait_recv()
+    c_copies["dh"] = send_coef(cbuf.at[2, high], 6, high, 5, across_y)
+    c_copies["y0"].wait_recv()
+    c_copies["y1"].wait_recv()
+    c_copies["dl"] = send_coef(cbuf.at[4, low], 6, low, 6, across_x)
+    lax.fori_loop(blocks, 2 * blocks, add_term, 0)
 
     c_copies["xl"].wait_recv()
     c_copies["sx"] = send_coef(cbuf.at[2], 3, pl.ds(0, NSH), 7, sibling)
@@ -159,6 +249,8 @@
 
     lax.fori_loop(0, NSH // 2, place, 0)
 
+    left_copy = pltpu.make_async_copy(left, left_out, l_sem)
+    left_copy.start()
     out_copies = [None, None]
     height = 2 * width
 
@@ -178,33 +270,26 @@
             return 0
 
         lax.fori_loop(0, rows // 2, tile, 0)
-        source = me
-        for bit in (1, 2, 4):
-            if slot & bit:
-                source = source + flip(bit) - me
-        columns = pl.ds(pl.multiple_of(source * width, width), width)
-        copy = pltpu.make_async_copy(stage.at[buf], out.at[:, :, columns], o_sem.at[buf])
+        copy = pltpu.make_async_copy(stage.at[buf], out.at[step], o_sem.at[buf])
         copy.start()
         out_copies[buf] = copy
 
-    panel(0, 0)
+    panel(0, FIRST[0])
     c_copies["s"].wait_recv()
-    panel(1, 1)
-    panel(2, 2)
+    panel(1, FIRST[1])
     c_copies["dh"].wait_recv()
     c_copies["dl"].wait_recv()
     c_copies["sd"] = send_coef(cbuf.at[6], 7, pl.ds(0, NSH), 9, sibling)
-    panel(3, 4)
-    c_copies["sx"].wait_recv()
-    panel(4, 3)
-    c_copies["sy"].wait_recv()
-    panel(5, 5)
-    panel(6, 6)
-    c_copies["sd"].wait_recv()
-    panel(7, 7)
+    panel(2, FIRST[2])
+    panel(3, FIRST[3])
+    for name in ("sx", "sy", "sd"):
+        c_copies[name].wait_recv()
+    coef_copies = [pltpu.make_async_copy(cbuf.at[slot], coefs_out.at[n], k_sem.at[n]) for n, slot in enumerate(SECOND)]
+    for copy in coef_copies:
+        copy.start()
     for copy in c_copies.values():
         copy.wait_send()
-    for copy in out_copies:
+    for copy in coef_copies + out_copies + [left_copy]:
         copy.wait()
 
 
@@ -212,24 +297,36 @@
     width = coef_act.shape[1]
     blocks = shell_pairs.shape[0]
     me = lax.axis_index("mo").astype(jnp.int32)
-    number = jnp.arange(blocks, dtype=jnp.int32)
-    slot = jnp.bitwise_xor(number % 8, me) * 4 + number // 8
-    terms, last = term_order(shell_pairs, slot)
-    pair_coef = jnp.stack([pair_coefficients(occ_lam, occ_sig, slabs[k]) for k in range(2)], axis=1)
+    here = me.reshape(1)
     rows = 2 * NI
+    vmem = pl.BlockSpec(memory_space=pltpu.VMEM)
+    smem = pl.BlockSpec(memory_space=pltpu.SMEM)
+    hbm = pl.BlockSpec(memory_space=pl.ANY)
+    terms, last, pair_coef = pl.pallas_call(
+        prepare_kernel,
+        out_shape=(
+            jax.ShapeDtypeStruct((3, 2 * blocks), jnp.int32),
+            jax.ShapeDtypeStruct((2, NSH), jnp.int32),
+            jax.ShapeDtypeStruct((4 * rows, KL * KS), jnp.bfloat16),
+        ),
+        in_specs=[smem, smem, vmem, vmem, vmem],
+        out_specs=(vmem, vmem, vmem),
+    )(slabs, here, shell_pairs, occ_lam, occ_sig)
     half = jnp.einsum(
         "mnw,jrw->jmrn", pair_ints.reshape(SH, SH, KL * KS), pair_coef.reshape(4, rows, KL * KS),
         preferred_element_type=jnp.float32,
     ).astype(jnp.bfloat16).reshape(4, SH, rows * SH)
     coef = coef_act.reshape(NSH, SH, width)
     dma = pltpu.SemaphoreType.DMA
-    vmem = pl.BlockSpec(memory_space=pltpu.VMEM)
-    smem = pl.BlockSpec(memory_space=pltpu.SMEM)
-    result = pl.pallas_call(
+    left, coefs, done = pl.pallas_call(
         fused_kernel,
-        out_shape=jax.ShapeDtypeStruct((rows, width, ACT), jnp.bfloat16),
+        out_shape=(
+            jax.ShapeDtypeStruct((rows * width, NSH * SH), jnp.bfloat16),
+            jax.ShapeDtypeStruct((4, NSH, SH, width), jnp.bfloat16),
+            jax.ShapeDtypeStruct((4, rows, width, width), jnp.bfloat16),
+        ),
         in_specs=[smem, smem, vmem, vmem],
-        out_specs=pl.BlockSpec(memory_space=pl.ANY),
+        out_specs=(hbm, hbm, hbm),
         scratch_shapes=[
             pltpu.VMEM((2 * blocks, SH, rows * SH), jnp.bfloat16),
             pltpu.VMEM((8, NSH, SH, width), jnp.bfloat16),
@@ -237,15 +334,32 @@
             pltpu.VMEM((2 * blocks, width, rows * SH), jnp.bfloat16),
             pltpu.VMEM((rows * width, NSH * SH), jnp.bfloat16),
             pltpu.VMEM((2, rows, width, width), jnp.bfloat16),
-            dma((3,)), dma((3,)), dma((7,)), dma((7,)), dma((10,)), dma((10,)), dma((2,)),
+            dma((3,)), dma((3,)), dma((7,)), dma((7,)), dma((12,)), dma((12,)), dma((2,)),
+            dma, dma((4,)),
         ],
         compiler_params=pltpu.CompilerParams(
             collective_id=0, has_side_effects=True, vmem_limit_bytes=56 * 2 ** 20
         ),
         cost_estimate=pl.CostEstimate(
-            flops=2 * rows * width * ACT * ACT, bytes_accessed=12 * 2 ** 20, transcendentals=0
+            flops=rows * width * ACT * ACT, bytes_accessed=12 * 2 ** 20, transcendentals=0
         ),
     )(terms, last, half, coef)
+    result = pl.pallas_call(
+        rest_kernel,
+        out_shape=jax.ShapeDtypeStruct((rows, width, ACT), jnp.bfloat16),
+        in_specs=[smem, hbm, hbm, hbm],
+        out_specs=hbm,
+        scratch_shapes=[
+            pltpu.VMEM((rows // 2, 2 * width, NSH * SH), jnp.bfloat16),
+            pltpu.VMEM((4, NSH * SH, width), jnp.bfloat16),
+            pltpu.VMEM((rows // 2, 4, 2, width, width), jnp.bfloat16),
+            dma((rows // 2,)), dma((4,)), dma((4,)), dma((rows // 2, 4)),
+        ],
+        compiler_params=pltpu.CompilerParams(vmem_limit_bytes=56 * 2 ** 20),
+        cost_estimate=pl.CostEstimate(
+            flops=rows * width * ACT * ACT, bytes_accessed=24 * 2 ** 20, transcendentals=0
+        ),
+    )(here, left, coefs.reshape(4, NSH * SH, width), done)
     return result.reshape(2, 1, NI, width, ACT)
 
 

time: 105 us -> 202 us (1.92)
  Pallas kernels: 84.7 us -> 195 us
  local copies, waits for them, and re-layouts: 13 us -> 5.33 us
  other arithmetic: 4.81 us -> 0 us
    pallas_call x1 -> x3, Pallas kernels: 84.7 us -> 195 us  [the longest x1 128 us: fused_body(): pl.pallas_call(rest_kernel, out_shape=jax.ShapeDtypeStruct((rows, width,...]
    unnamed x3 -> x4, local copies, waits for them, and re-layouts: 10 us -> 4.31 us
where the time goes in v2:
time: 202 us
  Pallas kernels  195 us (97%)
  local copies, waits for them, and re-layouts  5.33 us (3%)
    pallas_call x1, Pallas kernels, fused_body(): pl.pallas_call(rest_kernel, out_shape=jax.ShapeDtypeStruct((rows, width,...  128 us
    pallas_call x1, Pallas kernels, fused_body(): pl.pallas_call(fused_kernel, out_shape=(jax.ShapeDtypeStruct((rows * widt...  64.5 us
    unnamed x4, local copies, waits for them, and re-layouts  4.31 us

profile of v2, /device:TPU:0, one launch (start us, length us, event | category | flops | bytes accessed | tf_op | source)
XLA Modules:
  0.0 201.9 jit_solution(17387967581324460349)
XLA Ops:
  0.0 0.0 copy-start
  0.0 1.6 copy-done
  1.6 1.4 copy.8.occ_sig
  2.9 1.4 copy.7.pairs
  4.3 1.8 shard_map.64
  6.1 1.8 fusion
  7.9 1.0 reshape.24.half
  8.9 64.5 %shard_map.65 = (bf16[2048,2048]{1,0:T(8,128)(2,1)}, bf16[4,32,64,256]{3,2,1,0:T(8,128)(2,1)}, bf16[4,8,256,256]{3,2,1,0:T(8,128)(2,1)}) custom-call(s32[3,64]{1,0:T(4,128)} %get-tuple-element.11.terms, s32[2,32]{1,0:T(2,128)} %get-tuple-element.12.last, bf16[4,64,512]{2,1,0:T(8,128)(2,1)} %reshape.24.half, bf16[32,64,256]{2,1,0:T(8,128)(2,1)} %bitcast.22), custom_call_target="tpu_custom_call" | custom-call | flops 8589934592 | bytes 12582912 | tf_op jit(solution)/shard_map/pallas_call | solution.py:321
  73.4 128.4 %shard_map.66 = bf16[8,256,2048]{2,1,0:T(8,128)(2,1)} custom-call(s32[1]{0:T(128)} %bitcast.me, bf16[2048,2048]{1,0:T(8,128)(2,1)} %get-tuple-element.14.left, bf16[4,2048,256]{2,1,0:T(8,128)(2,1)} %bitcast.23, bf16[4,8,256,256]{3,2,1,0:T(8,128)(2,1)} %get-tuple-element.16.done), custom_call_target="tpu_custom_call" | custom-call | flops 8589934592 | bytes 25165824 | tf_op jit(solution)/shard_map/pallas_call | solution.py:347
Async XLA Ops:
  0.0 1.6 copy-start

commit v3 on v2

--- a/solution.py
+++ b/solution.py
@@ -26,10 +26,16 @@
 
 
 def prepare_kernel(slabs, me, pairs, occ_lam, occ_sig, terms, last, pair_coef):
-    blocks = pairs.shape[0]
+    blocks = pairs.shape[1]
     count = 2 * blocks
-    numbers = pairs[...]
-    one, two = numbers[:, 0:1], numbers[:, 1:2]
+    numbers = pairs[...].astype(jnp.float32)
+    diagonal = lax.broadcasted_iota(jnp.int32, (blocks, blocks), 0) == lax.broadcasted_iota(
+        jnp.int32, (blocks, blocks), 1
+    )
+    one, two = (
+        jnp.sum(jnp.where(diagonal, numbers[n:n + 1, :], 0.0), axis=1, keepdims=True).astype(jnp.int32)
+        for n in range(2)
+    )
     block = lax.broadcasted_iota(jnp.int32, (blocks, 1), 0)
     slot = jnp.bitwise_xor(lax.rem(block, 8), jnp.full((blocks, 1), me[0], jnp.int32)) * 4 + block // 8
     real = jnp.float32
@@ -56,12 +62,13 @@
     last[1:2, :] = jnp.minimum(has, 1.0).astype(jnp.int32)
 
     rows, occupied = pair_coef.shape[0], occ_lam.shape[1]
-    nj_all = occ_sig.shape[1]
+    nj_all = occ_sig.shape[0]
     half = jnp.bfloat16
 
-    def pick(chosen, values, spread):
+    def pick(chosen, values, spread, contract):
         some = lax.dot_general(
-            jnp.where(chosen, 1.0, 0.0).astype(half), values, (((1,), (1,)), ((), ())), preferred_element_type=real
+            jnp.where(chosen, 1.0, 0.0).astype(half), values, (((1,), (contract,)), ((), ())),
+            preferred_element_type=real,
         )
         return jnp.dot(some.astype(half), jnp.where(spread, 1.0, 0.0).astype(half), preferred_element_type=real)
 
@@ -72,12 +79,12 @@
     column_j = lax.broadcasted_iota(jnp.int32, (rows, nj_all), 1)
     pair = lax.broadcasted_iota(jnp.int32, (KL, KL * KS), 1)
     single = lax.broadcasted_iota(jnp.int32, (KL, KL * KS), 0)
-    lam = pick(column == wanted, occ_lam[...], pair // KS == single)
-    sig = pick(column_j == row_j // (2 * NI), occ_sig[...], lax.rem(pair, KS) == single)
+    lam = pick(column == wanted, occ_lam[...], pair // KS == single, 1)
+    sig = pick(column_j == row_j // (2 * NI), occ_sig[...], lax.rem(pair, KS) == single, 0)
     pair_coef[...] = (lam * sig).astype(half)
 
 
-def rest_kernel(me, left, coefs, done, out, lbuf, cbuf, stage, l_sem, c_sem, d_sem, o_sem):
+def rest_kernel(me, left, coefs, done, out, lbuf, cbuf, dbuf, stage, l_sem, c_sem, d_sem, m_sem, o_sem):
     width = cbuf.shape[2]
     rows = done.shape[1]
     height = 2 * width
@@ -93,11 +100,11 @@
     lefts[0].start()
     for copy in loads[1:] + lefts[1:]:
         copy.start()
+    fetches = [pltpu.make_async_copy(done.at[n], dbuf.at[n], d_sem.at[n]) for n in range(4)]
     moves = [
-        pltpu.make_async_copy(done.at[n], out.at[:, :, columns(slot)], d_sem.at[n])
-        for n, slot in enumerate(FIRST)
+        pltpu.make_async_copy(dbuf.at[n], out.at[:, :, columns(slot)], m_sem.at[n]) for n, slot in enumerate(FIRST)
     ]
-    for copy in moves:
+    for copy in fetches:
         copy.start()
     stores = []
     for m in range(rows // 2):
@@ -112,13 +119,17 @@
             )
             copy.start()
             stores.append(copy)
+        if m < 2:
+            for n in (2 * m, 2 * m + 1):
+                fetches[n].wait()
+                moves[n].start()
     for copy in moves + stores:
         copy.wait()
 
 
 def fused_kernel(
     terms, last, half, coef, left_out, coefs_out, out,
-    hbuf, cbuf, carry, sums, left, stage,
+    hbuf, cbuf, coef_t, carry, sums, left, stage,
     hz_send, hz_recv, h_send, h_recv, c_send, c_recv, o_sem, l_sem, k_sem,
 ):
     z = lax.axis_index("ao")
@@ -172,6 +183,12 @@
     c_copies["x2"] = send_coef(coef.at[parts[2]], 2, parts[2], 0, across_x)
     c_copies["y0"] = send_coef(coef.at[parts[0]], 4, parts[0], 1, across_y)
     hbuf[z] = half[z]
+
+    def turn_coef(shell, _):
+        coef_t[shell] = coef[shell].astype(jnp.float32).T.astype(jnp.bfloat16)
+        return 0
+
+    lax.fori_loop(0, NSH // 2, turn_coef, 0)
     for copy in z_copies:
         copy.wait()
 
@@ -186,6 +203,7 @@
     h_y = send_half(0, 4, 3, across_y)
     h_s = send_half(0, 1, 0, sibling)
     c_copies["s"] = send_coef(coef, 1, pl.ds(0, NSH), 4, sibling)
+    lax.fori_loop(NSH // 2, NSH, turn_coef, 0)
     turn_slot(0)
     h_s.wait_recv()
     turn_slot(1)
@@ -213,9 +231,7 @@
     carry[...] = jnp.zeros_like(carry)
 
     def add_term(t, _):
-        added = lax.dot_general(
-            coef[terms[0, t]], hbuf[terms[1, t]], (((0,), (0,)), ((), ())), preferred_element_type=jnp.float32
-        )
+        added = jnp.dot(coef_t[terms[0, t]], hbuf[terms[1, t]], preferred_element_type=jnp.float32)
         total = jnp.where(terms[2, t] > 0, carry[...], 0.0) + added
         carry[...] = total
         sums[t] = total.astype(jnp.bfloat16)
@@ -311,7 +327,7 @@
         ),
         in_specs=[smem, smem, vmem, vmem, vmem],
         out_specs=(vmem, vmem, vmem),
-    )(slabs, here, shell_pairs, occ_lam, occ_sig)
+    )(slabs, here, shell_pairs.T, occ_lam, occ_sig.T)
     half = jnp.einsum(
         "mnw,jrw->jmrn", pair_ints.reshape(SH, SH, KL * KS), pair_coef.reshape(4, rows, KL * KS),
         preferred_element_type=jnp.float32,
@@ -330,6 +346,7 @@
         scratch_shapes=[
             pltpu.VMEM((2 * blocks, SH, rows * SH), jnp.bfloat16),
             pltpu.VMEM((8, NSH, SH, width), jnp.bfloat16),
+            pltpu.VMEM((NSH, width, SH), jnp.bfloat16),
             pltpu.VMEM((width, rows * SH), jnp.float32),
             pltpu.VMEM((2 * blocks, width, rows * SH), jnp.bfloat16),
             pltpu.VMEM((rows * width, NSH * SH), jnp.bfloat16),
@@ -352,8 +369,9 @@
         scratch_shapes=[
             pltpu.VMEM((rows // 2, 2 * width, NSH * SH), jnp.bfloat16),
             pltpu.VMEM((4, NSH * SH, width), jnp.bfloat16),
+            pltpu.VMEM((4, rows, width, width), jnp.bfloat16),
             pltpu.VMEM((rows // 2, 4, 2, width, width), jnp.bfloat16),
-            dma((rows // 2,)), dma((4,)), dma((4,)), dma((rows // 2, 4)),
+            dma((rows // 2,)), dma((4,)), dma((4,)), dma((4,)), dma((rows // 2, 4)),
         ],
         compiler_params=pltpu.CompilerParams(vmem_limit_bytes=56 * 2 ** 20),
         cost_estimate=pl.CostEstimate(

time: 202 us -> 85.5 us (0.42)
  Pallas kernels: 195 us -> 80.8 us
  local copies, waits for them, and re-layouts: 5.33 us -> 2.62 us
    pallas_call x1, Pallas kernels: 128 us -> 15 us  [fused_body(): pl.pallas_call(rest_kernel, out_shape=jax.ShapeDtypeStruct((rows, width,...]
    unnamed x4 -> x2, local copies, waits for them, and re-layouts: 4.31 us -> 1.59 us
where the time goes in v3:
time: 85.5 us; the launch traced here: 85.2 us
  Pallas kernels  80.8 us (95%)
  local copies, waits for them, and re-layouts  2.62 us (3%)
  matrix products  1.78 us (2%)
    pallas_call x1, Pallas kernels, fused_body(): pl.pallas_call(fused_kernel, out_shape=(jax.ShapeDtypeStruct((rows * widt...  64 us
    pallas_call x1, Pallas kernels, fused_body(): pl.pallas_call(rest_kernel, out_shape=jax.ShapeDtypeStruct((rows, width,...  15 us
    pallas_call x1, Pallas kernels, fused_body(): pl.pallas_call(prepare_kernel, out_shape=(jax.ShapeDtypeStruct((3, 2 * bl...  1.81 us
    dot_general x1, matrix products, fused_body(): jnp.einsum('mnw,jrw->jmrn', pair_ints.reshape(SH, SH, KL * KS), pair_coef...  1.78 us

profile of v3, /device:TPU:0, one launch (start us, length us, event | category | flops | bytes accessed | tf_op | source)
XLA Modules:
  0.0 85.2 jit_solution(5157563594034549629)
XLA Ops:
  0.0 0.0 copy-start
  0.0 1.6 %copy-done = bf16[1,4096,256]{2,1,0:T(8,128)(2,1)S(1)} copy-done((bf16[1,4096,256]{2,1,0:T(8,128)(2,1)S(1)}, bf16[1,4096,256]{2,1,0:T(8,128)(2,1)}, u32[]{:S(2)}) %copy-start) | copy-done | bytes 2097176
  1.6 1.8 %shard_map.64 = (s32[3,64]{1,0:T(4,128)}, s32[2,32]{1,0:T(2,128)}, bf16[32,256]{1,0:T(8,128)(2,1)}) custom-call(s32[2]{0:T(128)} %slabs.1, s32[1]{0:T(128)} %bitcast.me, s32[2,32]{1,0:T(2,128)} %bitcast.24, bf16[16,32]{1,0:T(8,128)(2,1)} %occ_lam.1, bf16[4,16]{1,0:T(4,128)(2,1)} %bitcast.25), custom_call_target="tpu_custom_call" | custom-call | tf_op jit(solution)/shard_map/pallas_call | solution.py:321
  3.4 1.8 %fusion = bf16[4,64,8,64]{3,2,1,0:T(8,128)(2,1)S(1)} fusion(bf16[64,64,256,1]{2,1,0,3:T(8,128)(2,1)S(1)} %bitcast.23, bf16[32,256]{1,0:T(8,128)(2,1)} %get-tuple-element.13), kind=kOutput, calls=%fused_computation.1 | convolution fusion | flops 67239936 | bytes 2375680 | tf_op jit(solution)/shard_map/mnw,jrw->jmrn/dot_general | solution.py:331
  5.2 1.0 %reshape.24.half = bf16[4,64,512]{2,1,0:T(8,128)(2,1)} reshape(bf16[4,64,8,64]{3,2,1,0:T(8,128)(2,1)S(1)} %fusion) | data formatting | bytes 524288 | tf_op jit(solution)/shard_map/reshape | solution.py:334
  6.2 64.0 %shard_map.65 = (bf16[2048,2048]{1,0:T(8,128)(2,1)}, bf16[4,32,64,256]{3,2,1,0:T(8,128)(2,1)}, bf16[4,8,256,256]{3,2,1,0:T(8,128)(2,1)}) custom-call(s32[3,64]{1,0:T(4,128)} %get-tuple-element.11.terms, s32[2,32]{1,0:T(2,128)} %get-tuple-element.12.last, bf16[4,64,512]{2,1,0:T(8,128)(2,1)} %reshape.24.half, bf16[32,64,256]{2,1,0:T(8,128)(2,1)} %bitcast.26), custom_call_target="tpu_custom_call" | custom-call | flops 8589934592 | bytes 12582912 | tf_op jit(solution)/shard_map/pallas_call | solution.py:337
  70.2 15.0 %shard_map.66 = bf16[8,256,2048]{2,1,0:T(8,128)(2,1)} custom-call(s32[1]{0:T(128)} %bitcast.me, bf16[2048,2048]{1,0:T(8,128)(2,1)} %get-tuple-element.14.left, bf16[4,2048,256]{2,1,0:T(8,128)(2,1)} %bitcast.27, bf16[4,8,256,256]{3,2,1,0:T(8,128)(2,1)} %get-tuple-element.16.done), custom_call_target="tpu_custom_call" | custom-call | flops 8589934592 | bytes 25165824 | tf_op jit(solution)/shard_map/pallas_call | solution.py:364
Async XLA Ops:
  0.0 1.6 %copy-start = (bf16[1,4096,256]{2,1,0:T(8,128)(2,1)S(1)}, bf16[1,4096,256]{2,1,0:T(8,128)(2,1)}, u32[]{:S(2)}) copy-start(bf16[1,4096,256]{2,1,0:T(8,128)(2,1)} %param.6) | copy-start | bytes 6291460
